TPU v7x, 32 devices: a whole 2x2x4 slice. The times are simulated.
32 devices in a mesh: mem: 8 (over z, x), pb: 4 (over y, core).
Axes of the slice: x: 2, y: 2, z: 4, core: 2. Of those that a mesh axis runs over, the one named last changes fastest.
Arguments:
- queries: bfloat16 [4096, 1024], P(('pb', 'mem')), may hold values from -9 to 9
- local_keys: bfloat16 [4096, 1024], P(('pb', 'mem')), may hold values from -9 to 9
- local_values: bfloat16 [4096, 1024], P(('pb', 'mem')), may hold values from -6 to 6
- memory_keys: bfloat16 [8192, 1024], P('mem'), may hold values from -11 to 11
- memory_values: bfloat16 [8192, 1024], P('mem'), may hold values from -6 to 6
- neighbour_index_rows: int32 [4096, 32], P(('pb', 'mem')), may hold values from 0 to 8191, as said below
- gate_bias: float32 [8], replicated, may hold values from -2.5 to 2.5
- out_weight: bfloat16 [1024, 1024], P('pb'), may hold values from -0.75 to 0.75
Outputs:
- layer_out: bfloat16 [4096, 1024], P(('pb', 'mem'))
Inputs may be any that keep to these rules, and one draw needn't show every extreme that they name: `neighbour_index_rows`: memory shard o holds rows o * 1024 to (o + 1) * 1024 - 1. Among the 4096 ids of one device's rows, at most 1024 fall in any one shard, and exactly 1024 fall in some shard; for each index of pb, one shard receives exactly 1024 from every device with that index. Ids of a row may repeat.
All inputs are finite; a program needn't handle non-finite values.
Results may differ from a plain program's by a relative error of at most 0.01.
Values may be sent and summed in bfloat16 or wider, within the bound.
A program may use at most 192 MiB of HBM per device.

v0:
```python
import math
import jax
import jax.numpy as jnp
from jax import lax
from jax.sharding import PartitionSpec as P


def combined_all(value, axis, join):
    pieces = jax.tree.map(lambda part: lax.all_gather(part, axis), value)
    head = jax.tree.map(lambda part: part[0], pieces)
    tail = jax.tree.map(lambda part: part[1:], pieces)
    subtotal, _ = lax.scan(lambda subtotal, share: (join(subtotal, share), None), head, tail)
    return subtotal


def join_totals(first, second):
    peak = jnp.maximum(first[0], second[0])
    return (peak, first[1] * jnp.exp(first[0] - peak) + second[1] * jnp.exp(second[0] - peak))


def slot_ranks(owners, count):
    onehot = (owners[:, None] == jnp.arange(count, dtype=jnp.int32)[None, :]).astype(jnp.int32)
    return jnp.sum(jnp.cumsum(onehot, axis=0) * onehot, axis=1) - 1


def body(
    queries,
    local_keys,
    local_values,
    memory_keys,
    memory_values,
    neighbour_index_rows,
    gate_bias,
    out_weight,
):
    shard_count = lax.axis_size("mem")
    my_shard = lax.axis_index("mem")
    row_count = queries.shape[0]
    model_width = queries.shape[1]
    head_count = gate_bias.shape[0]
    head_size = model_width // head_count
    memory_rows = memory_keys.shape[0]
    top_count = neighbour_index_rows.shape[1]
    capacity = 2 * row_count * top_count // shard_count
    group_rows = shard_count * row_count
    multiplier = head_size ** (-0.5)
    row_numbers = jnp.arange(row_count, dtype=jnp.int32)
    group_queries = lax.all_gather(queries, "mem", axis=0, tiled=True)
    query_heads = queries.reshape(row_count, head_count, head_size)
    key_local = local_keys.reshape(row_count, head_count, head_size)
    value_local = local_values.reshape(row_count, head_count, head_size)
    local_scores = (
        jnp.einsum("qhd,khd->hqk", query_heads, key_local, preferred_element_type=jnp.float32)
        * multiplier
    )
    causal = row_numbers[:, None] >= row_numbers[None, :]
    local_scores = jnp.where(causal[None], local_scores, -jnp.inf)
    local_peak = jnp.max(local_scores, axis=-1, keepdims=True)
    local_expo = jnp.exp(local_scores - local_peak)
    local_weights = (local_expo / jnp.sum(local_expo, axis=-1, keepdims=True)).astype(jnp.bfloat16)
    local_out = jnp.einsum(
        "hqk,khd->qhd", local_weights, value_local, preferred_element_type=jnp.float32
    )
    key_head_count = memory_keys.reshape(memory_rows, head_count, head_size)
    block = math.gcd(group_rows, 512)

    def block_stats(query_tile_block):
        reshaped_tensor = query_tile_block.reshape(block, head_count, head_size)
        logit_scores = (
            jnp.einsum(
                "bvt,yvt->bvy", reshaped_tensor, key_head_count, preferred_element_type=jnp.float32
            )
            * multiplier
        )
        block_peak = jnp.max(logit_scores, axis=2)
        return (block_peak, jnp.sum(jnp.exp(logit_scores - block_peak[:, :, None]), axis=2))

    peaks, totals = lax.map(
        block_stats, group_queries.reshape(group_rows // block, block, model_width)
    )
    peaks = peaks.reshape(group_rows, head_count)
    totals = totals.reshape(group_rows, head_count)
    global_peak, global_total = combined_all((peaks, totals), "mem", join_totals)
    source_queries = group_queries.reshape(shard_count, row_count, head_count, head_size)
    source_peaks = global_peak.reshape(shard_count, row_count, head_count)
    flat_ids = neighbour_index_rows.reshape(-1)
    entry_row_list = jnp.arange(row_count * top_count, dtype=jnp.int32) // top_count
    owners = flat_ids // memory_rows
    ranks = slot_ranks(owners, shard_count)
    codes = entry_row_list * memory_rows + flat_ids % memory_rows
    slots = owners * capacity + ranks
    requests = (
        jnp.full((shard_count * capacity,), -1, jnp.int32)
        .at[slots]
        .set(codes)
        .reshape(shard_count, capacity)
    )
    slot_owner_row = (
        jnp.full((shard_count * capacity,), -1, jnp.int32).at[slots].set(entry_row_list)
    )
    codes = lax.all_to_all(requests, "mem", split_axis=0, concat_axis=0, tiled=True)
    valid = codes >= 0
    safe = jnp.where(valid, codes, 0)
    offsets = safe % memory_rows
    local_rows = jnp.where(valid, safe // memory_rows, -1)
    slot_width = codes.shape[1]
    picked_keys = memory_keys[offsets].reshape(codes.shape[0], slot_width, head_count, head_size)
    values = memory_values[offsets]

    def score_source(inputs):
        query_block, key_block, rows_here, peak_block = inputs
        full = (
            jnp.einsum("qhd,chd->hqc", query_block, key_block, preferred_element_type=jnp.float32)
            * multiplier
        )
        hit = rows_here[None, :] == row_numbers[:, None]
        scores = jnp.sum(jnp.where(hit[None], full, 0.0), axis=1)
        peak_here = jnp.sum(jnp.where(hit[:, :, None], peak_block[:, None, :], 0.0), axis=0)
        weight_here = jnp.exp(scores.T - peak_here)
        return jnp.where((rows_here >= 0)[:, None], weight_here, 0.0).astype(jnp.bfloat16)

    weights = lax.map(score_source, (source_queries, picked_keys, local_rows, source_peaks))
    weights, values, local_rows = (weights, values, local_rows)
    values, weights = (
        lax.all_to_all(values, "mem", split_axis=0, concat_axis=0, tiled=True),
        lax.all_to_all(weights, "mem", split_axis=0, concat_axis=0, tiled=True),
    )
    flat_values = values.reshape(shard_count * capacity, head_count, head_size)
    flat_weights = weights.reshape(shard_count * capacity, head_count)
    hit = slot_owner_row[None, :] == row_numbers[:, None]
    scaled = jnp.where(hit[None], flat_weights.T[:, None, :], jnp.zeros((), jnp.bfloat16))
    numerator = jnp.einsum("hqs,shd->qhd", scaled, flat_values, preferred_element_type=jnp.float32)
    denominator = jnp.dot(
        hit.astype(jnp.bfloat16), flat_weights, preferred_element_type=jnp.float32
    )
    own_total = lax.dynamic_slice_in_dim(global_total, my_shard * row_count, row_count, 0)
    background = top_count / (memory_rows * shard_count) * own_total
    memory_out = numerator / (denominator + background)[:, :, None]
    gate = jax.nn.sigmoid(gate_bias)[None, :, None]
    mixed = (
        (gate * memory_out + (1.0 - gate) * local_out)
        .reshape(row_count, model_width)
        .astype(jnp.bfloat16)
    )
    result = jnp.dot(
        mixed,
        lax.all_gather(out_weight, "pb", axis=0, tiled=True),
        preferred_element_type=jnp.float32,
    )
    return result.astype(jnp.bfloat16)


def solution(mesh):
    in_specs = (
        P(("pb", "mem"), None),
        P(("pb", "mem"), None),
        P(("pb", "mem"), None),
        P("mem", None),
        P("mem", None),
        P(("pb", "mem"), None),
        P(),
        P("pb", None),
    )
    out_specs = P(("pb", "mem"), None)
    return jax.shard_map(body, mesh=mesh, in_specs=in_specs, out_specs=out_specs, check_vma=False)
```

profile of v0, /device:TPU:0, one launch (start us, length us, event | category | flops | bytes accessed | tf_op | source)
XLA Modules:
  0.0 718.5 jit_solution(11344651262773590090)
XLA Ops:
  9.2 2.3 reduce-window.6
  12.4 16.1 %scatter_custom_fusion = s32[8192]{0:T(1024)} fusion(s32[4096]{0:T(1024)S(1)} %bitcast.179, s32[4096]{0:T(1024)S(1)} %get-tuple-element.207, s32[]{:T(128)} %constant.123.clone.1), kind=kCustom, calls=%fused_computation.112 | custom fusion | bytes 32772 | tf_op jit(solution)/shard_map/scatter | solution.py:95
  28.5 7.3 %all-to-all-start = ((s32[8,1,1024]{2,1,0:T(1,128)}), s32[8,1,1024]{2,1,0:T(1,128)S(1)}, u32[]{:S(2)}, u32[]{:S(2)}) async-start(s32[8,1,1024]{2,1,0:T(1,128)} %bitcast.9), calls=%async_computation | async-start | bytes 65536 | tf_op jit(solution)/shard_map/all_to_all | solution.py:101
  35.8 4.0 copy.67
  39.7 3.9 copy.69
  43.8 42.5 %gather_fusion.1 = bf16[8192,1024]{1,0:T(8,128)(2,1)} fusion(bf16[1024,1024]{1,0:T(8,128)(2,1)} %param.17, s32[8192]{0:T(1024)S(1)} %broadcast_clamp_fusion), kind=kCustom, calls=%fused_computation.1 | custom fusion | bytes 33587200 | tf_op jit(solution)/shard_map/gather | solution.py:107
  86.3 15.6 %copy.87 = bf16[1024,8,8,128]{3,2,1,0:T(8,128)(2,1)} copy(bf16[1024,8,8,128]{3,1,2,0:T(8,128)(2,1)} %bitcast.161) | data formatting | bytes 33554432
  102.0 23.2 %while.35 = (s32[]{:T(128)}, f32[2,512,8]{1,2,0:T(8,128)S(1)}, f32[2,512,8]{1,2,0:T(8,128)S(1)}, bf16[2,512,1024]{2,1,0:T(8,128)(2,1)}, bf16[1024,8,128]{2,0,1:T(8,128)(2,1)}, /*index=5*/s32[]{:T(128)}) while((s32[]{:T(128)}, f32[2,512,8]{1,2,0:T(8,128)S(1)}, f32[2,512,8]{1,2,0:T(8,128)S(1)}, bf16[2,512,1024]{2,1,0:T(8,128)(2,1)}, ...), condition=%wide.region_8.9_spmd, body=%wide.region_5.8_spmd.sunk | while | flops 1094705152 | bytes 41009228 | solution.py:78
  102.0 2.3 constant_dynamic-slice_fusion.8
  105.8 4.2 bitcast_reduce_fusion.2
  110.1 3.5 fusion.76
  113.6 2.3 constant_dynamic-slice_fusion.8
  117.4 4.2 bitcast_reduce_fusion.2
  121.6 3.5 fusion.76
  125.2 31.4 %all_gather.14 = f32[8,1024,8]{1,2,0:T(8,128)S(1)} all-gather(f32[1,1024,8]{1,2,0:T(8,128)S(1)} %bitcast.177), channel_id=1, replica_groups=mesh['mem'=8,'pb'=4] {'mem'}, dimensions={0}, use_global_device_ids=true | all-gather | bytes 294912 | tf_op jit(solution)/shard_map/all_gather | solution.py:9
  156.6 30.7 %all_gather.13 = f32[8,1024,8]{1,2,0:T(8,128)S(1)} all-gather(f32[1,1024,8]{1,2,0:T(8,128)S(1)} %bitcast.176), channel_id=1, replica_groups=mesh['mem'=8,'pb'=4] {'mem'}, dimensions={0}, use_global_device_ids=true | all-gather | bytes 294912 | tf_op jit(solution)/shard_map/all_gather | solution.py:9
  187.8 3.6 copy.86
  191.4 43.2 %while.37 = (s32[]{:T(128)}, bf16[8,1024,8]{1,2,0:T(8,128)(2,1)}, s32[8,1024]{1,0:T(8,128)S(1)}, bf16[8,128,8,128]{3,2,1,0:T(8,128)(2,1)}, bf16[8,1024,8,128]{3,...) while((s32[]{:T(128)}, bf16[8,1024,8]{1,2,0:T(8,128)(2,1)}, ...), condition=%wide.region_14.15_spmd.clone, body=%wide.region_11.14_spmd.clone.sunk | while | flops 273818624 | bytes 7658077 | solution.py:122
  191.4 1.7 constant_dynamic-slice_fusion.10
  196.8 1.7 constant_dynamic-slice_fusion.10
  202.2 1.7 constant_dynamic-slice_fusion.10
  234.6 5.4 all-to-all-start.2
  239.9 35.4 %gather_fusion = bf16[8192,1024]{1,0:T(8,128)(2,1)} fusion(bf16[1024,1024]{1,0:T(8,128)(2,1)S(1)} %copy-done, s32[8192]{0:T(1024)S(1)} %broadcast_clamp_fusion), kind=kCustom, calls=%fused_computation | custom fusion | bytes 33587200 | tf_op jit(solution)/shard_map/gather | solution.py:108
  275.4 21.6 %copy.65 = bf16[8,1024,1024]{1,2,0:T(8,128)(2,1)} copy(bf16[8,1024,1024]{2,1,0:T(8,128)(2,1)} %bitcast.160) | data formatting | bytes 33554432 | tf_op jit(solution)/shard_map/gather | solution.py:108
  297.0 6.1 all-to-all-start.1
  303.7 15.7 %scatter_custom_fusion.1 = s32[8192]{0:T(1024)S(1)} fusion(s32[4096]{0:T(1024)} %bitcast.180, s32[4096]{0:T(1024)S(1)} %add_select_fusion.2, s32[]{:T(128)} %constant.123.clone.1), kind=kCustom, calls=%fused_computation.110 | custom fusion | bytes 33280 | tf_op jit(solution)/shard_map/scatter | solution.py:99
  322.1 331.0 %all-to-all-done.1 = bf16[8,1024,1024]{1,2,0:T(8,128)(2,1)} async-done(((bf16[8,1024,1024]{1,2,0:T(8,128)(2,1)}), bf16[8,1024,1024]{1,2,0:T(8,128)(2,1)}, u32[]{:S(2)}, u32[]{:S(2)}) %all-to-all-start.1) | async-done | bytes 16777248 | tf_op jit(solution)/shard_map/all_to_all | solution.py:125
  653.1 18.7 %copy.66 = bf16[8,1024,1024]{1,0,2:T(8,128)(2,1)} copy(bf16[8,1024,1024]{1,2,0:T(8,128)(2,1)} %all-to-all-done.1) | data formatting | bytes 33554432 | tf_op jit(solution)/shard_map/all_to_all | solution.py:125
  671.8 25.6 %reshape.338 = bf16[8192,8,128]{0,2,1:T(8,128)(2,1)} reshape(bf16[8,1024,1024]{1,0,2:T(8,128)(2,1)} %copy.66) | data formatting | bytes 33554432 | tf_op jit(solution)/shard_map/reshape | solution.py:128
  697.4 9.2 %fusion.29 = f32[128,8,128]{0,2,1:T(8,128)} fusion(bf16[8192,8,128]{0,2,1:T(8,128)(2,1)} %reshape.338, pred[128,8192]{1,0:T(8,128)(4,1)S(1)} %iota_compare_fusion.1, bf16[8,8192]{1,0:T(8,128)(2,1)S(1)} %bitcast.173, f32[128,8]{0,1:T(8,128)S(1)} %convolution_add_fusion, f32[8]{0:T(128)S(1)} %get-tuple-element.202), kind=kOutput, calls=%fused_computation.52 | convolution fusion | flops 2156134400 | bytes 18485280 | tf_op jit(solution)/shard_map/hqs,shd->qhd/dot_general | solution.py:132
  706.5 1.7 fusion.25
  708.3 2.8 convolution_convert_fusion
  (144 shorter events, 47.4 us)
Async XLA Ops:
  7.4 232.6 %copy-start = (bf16[1024,1024]{1,0:T(8,128)(2,1)S(1)}, bf16[1024,1024]{1,0:T(8,128)(2,1)}, u32[]{:S(2)}) copy-start(bf16[1024,1024]{1,0:T(8,128)(2,1)} %param.18) | copy-start | bytes 6291460
  7.4 94.7 %all-gather.3.cloned.1.call-start = ((), (), s32[]{:S(2)}) async-start(), calls=%async_computation.3 | async-start | bytes 2359296 | tf_op jit(solution)/shard_map/all_gather | solution.py:48
  12.4 31.3 %copy-start.5 = (s32[4096,1]{0,1:T(1,128)}, s32[4096,1]{0,1:T(1,128)S(1)}, u32[]{:S(2)}) copy-start(s32[4096,1]{0,1:T(1,128)S(1)} %compare_select_fusion.4) | copy-start | bytes 49156
  28.5 15.2 %all-to-all-start = ((s32[8,1,1024]{2,1,0:T(1,128)}), s32[8,1,1024]{2,1,0:T(1,128)S(1)}, u32[]{:S(2)}, u32[]{:S(2)}) async-start(s32[8,1,1024]{2,1,0:T(1,128)} %bitcast.9), calls=%async_computation | async-start | bytes 65536 | tf_op jit(solution)/shard_map/all_to_all | solution.py:101
  234.6 62.4 %all-to-all-start.2 = ((bf16[8,1024,8]{1,2,0:T(8,128)(2,1)}), bf16[8,1024,8]{1,2,0:T(8,128)(2,1)S(1)}, u32[]{:S(2)}, u32[]{:S(2)}) async-start(bf16[8,1024,8]{1,2,0:T(8,128)(2,1)} %get-tuple-element.101), calls=%async_computation.2 | async-start | bytes 262144 | tf_op jit(solution)/shard_map/all_to_all | solution.py:126
  296.9 22.5 %copy-start.3 = (bf16[128,1024]{1,0:T(8,128)(2,1)S(1)}, bf16[128,1024]{1,0:T(8,128)(2,1)}, u32[]{:S(2)}) copy-start(bf16[128,1024]{1,0:T(8,128)(2,1)} %param.16) | copy-start | bytes 786436
  296.9 23.3 %copy-start.4 = (bf16[128,1024]{1,0:T(8,128)(2,1)S(1)}, bf16[128,1024]{1,0:T(8,128)(2,1)}, u32[]{:S(2)}) copy-start(bf16[128,1024]{1,0:T(8,128)(2,1)} %param.14) | copy-start | bytes 786436
  296.9 23.3 %copy-start.6 = (bf16[128,1024]{1,0:T(8,128)(2,1)S(1)}, bf16[128,1024]{1,0:T(8,128)(2,1)}, u32[]{:S(2)}) copy-start(bf16[128,1024]{1,0:T(8,128)(2,1)} %param.15) | copy-start | bytes 786436
  296.9 23.8 %copy-start.7 = (f32[8]{0:T(128)S(1)}, f32[8]{0:T(128)}, u32[]{:S(2)}) copy-start(f32[8]{0:T(128)} %param.20) | copy-start | bytes 100
  297.0 356.1 %all-to-all-start.1 = ((bf16[8,1024,1024]{1,2,0:T(8,128)(2,1)}), bf16[8,1024,1024]{1,2,0:T(8,128)(2,1)}, u32[]{:S(2)}, u32[]{:S(2)}) async-start(bf16[8,1024,1024]{1,2,0:T(8,128)(2,1)} %copy.65), calls=%async_computation.1 | async-start | bytes 33554432 | tf_op jit(solution)/shard_map/all_to_all | solution.py:125
  303.1 405.2 %all-gather.5.cloned.1.call-start = ((), (), s32[]{:S(2)}) async-start(), calls=%async_computation.4 | async-start | bytes 2621440 | tf_op jit(solution)/shard_map/all_gather | solution.py:147
  320.6 351.2 %copy-start.2 = (f32[8,128,128]{1,2,0:T(8,128)}, f32[8,128,128]{1,2,0:T(8,128)S(1)}, u32[]{:S(2)}) copy-start(f32[8,128,128]{1,2,0:T(8,128)S(1)} %fusion.21) | copy-start | bytes 1572868
  697.4 13.7 %copy-start.1 = (bf16[1024,1024]{1,0:T(8,128)(2,1)S(1)}, bf16[1024,1024]{1,0:T(8,128)(2,1)}, u32[]{:S(2)}) copy-start(bf16[1024,1024]{1,0:T(8,128)(2,1)} %param.18) | copy-start | bytes 6291460
Sparse Core Ops, SparseCore 0:
  10.3 51.9 all-gather.2
Sparse Core Ops, SparseCore 1:
  305.1 23.8 all-gather.4
where the time goes:
time: 721 us; the launch traced here: 719 us
  waiting for transfers between devices  332 us (46%)
  local copies, waits for them, and re-layouts  235 us (33%)
  blocking collectives  62.1 us (9%)
  matrix products  32.6 us (5%)
  other arithmetic  21.9 us (3%)
  starting transfers between devices  18.8 us (3%)
  between operations  15.1 us (2%)
    all_to_all x1, waiting for transfers between devices, body(): lax.all_to_all(values, 'mem', split_axis=0, concat_axis=0, tiled=True)  331 us
    all_gather x2, blocking collectives, combined_all(): pieces = jax.tree.map(lambda part: lax.all_gather(part, axis), value)  62.1 us
    gather x2, local copies, waits for them, and re-layouts, body(): values = memory_values[offsets]  57 us
    gather x1, local copies, waits for them, and re-layouts, body(): memory_keys[offsets]  42.5 us
    reshape x1, local copies, waits for them, and re-layouts, body(): flat_values = values.reshape(shard_count * capacity, head_count, head_size)  25.6 us
    unnamed x20, local copies, waits for them, and re-layouts  24 us
    dynamic_slice x24, local copies, waits for them, and re-layouts, body(): lax.map(score_source, (source_queries, picked_keys, local_rows, source_pe...  21.7 us
    all_to_all x1, local copies, waits for them, and re-layouts, body(): lax.all_to_all(values, 'mem', split_axis=0, concat_axis=0, tiled=True)  18.7 us
  transfers between devices with their start and end apart: 5, of which 1 were waited for; matrix products, arithmetic and copies ran while one was open for 30% of the time, Pallas kernels for 0%

commit v1 on v0

--- a/solution.py
+++ b/solution.py
@@ -3,6 +3,30 @@
 import jax.numpy as jnp
 from jax import lax
 from jax.sharding import PartitionSpec as P
+
+
+def split_up(value, dim, length):
+    lengths = value.shape
+    blocks = value.reshape(*lengths[:dim], length, lengths[dim] // length, *lengths[dim + 1 :])
+    return jnp.moveaxis(blocks, dim, 0)
+
+
+def in_order(blocks, dim):
+    blocks = jnp.moveaxis(blocks, 0, dim)
+    shape = blocks.shape
+    return blocks.reshape(*shape[:dim], shape[dim] * shape[dim + 1], *shape[dim + 2 :])
+
+
+def sent_to_each(value, axis, split_dim, concat_dim):
+    count, position = (lax.axis_size(axis), lax.axis_index(axis))
+    pieces = split_up(value, split_dim, count)
+    out = pieces
+    for step in range(1, count):
+        target, source = ((position + step) % count, (position - step) % count)
+        sent = lax.dynamic_index_in_dim(pieces, target, 0)
+        other = lax.ppermute(sent, axis, [(i, (i + step) % count) for i in range(count)])
+        out = lax.dynamic_update_slice_in_dim(out, other, source, axis=0)
+    return in_order(out, concat_dim)
 
 
 def combined_all(value, axis, join):
@@ -122,7 +146,7 @@
     weights = lax.map(score_source, (source_queries, picked_keys, local_rows, source_peaks))
     weights, values, local_rows = (weights, values, local_rows)
     values, weights = (
-        lax.all_to_all(values, "mem", split_axis=0, concat_axis=0, tiled=True),
+        sent_to_each(values, "mem", 0, 0),
         lax.all_to_all(weights, "mem", split_axis=0, concat_axis=0, tiled=True),
     )
     flat_values = values.reshape(shard_count * capacity, head_count, head_size)

time: 721 us -> 657 us (0.911)
  waiting for transfers between devices: 332 us -> 153 us
  blocking collectives: 62.1 us -> 191 us
  local copies, waits for them, and re-layouts: 235 us -> 206 us
  starting transfers between devices: 18.8 us -> 31.8 us
    all_to_all x1 -> x0, waiting for transfers between devices: 331 us -> none  [body(): lax.all_to_all(values, 'mem', split_axis=0, concat_axis=0, tiled=True)]
    ppermute x0 -> x7, waiting for transfers between devices: none -> 149 us  [sent_to_each(): lax.ppermute(sent, axis, [(i, (i + step) % count) for i in range(count)])]
    all_gather x2, blocking collectives: 62.1 us -> 191 us  [combined_all(): pieces = jax.tree.map(lambda part: lax.all_gather(part, axis), value)]
    reshape x1 -> x0, local copies, waits for them, and re-layouts: 25.6 us -> none  [body(): flat_values = values.reshape(shard_count * capacity, head_count, head_size)]
    dynamic_update_slice x0 -> x7, local copies, waits for them, and re-layouts: none -> 21.7 us  [sent_to_each(): out = lax.dynamic_update_slice_in_dim(out, other, source, axis=0)]
    gather x2 -> x1, local copies, waits for them, and re-layouts: 57 us -> 35.4 us  [body(): values = memory_values[offsets]]
    all_to_all x1 -> x0, local copies, waits for them, and re-layouts: 18.7 us -> none  [body(): lax.all_to_all(values, 'mem', split_axis=0, concat_axis=0, tiled=True)]
    ppermute x0 -> x7, starting transfers between devices: none -> 18.5 us  [sent_to_each(): lax.ppermute(sent, axis, [(i, (i + step) % count) for i in range(count)])]
  transfers between devices with their start and end apart: 5 -> 11, of which waited for: 1 -> 3; matrix products, arithmetic and copies ran while one was open for 30% -> 40% of each run, Pallas kernels for 0% -> 0%
where the time goes in v1:
time: 657 us; the launch traced here: 655 us
  local copies, waits for them, and re-layouts  206 us (31%)
  blocking collectives  191 us (29%)
  waiting for transfers between devices  153 us (23%)
  matrix products  36.2 us (6%)
  starting transfers between devices  31.8 us (5%)
  other arithmetic  23.7 us (4%)
  between operations  13.6 us (2%)
    all_gather x2, blocking collectives, combined_all(): pieces = jax.tree.map(lambda part: lax.all_gather(part, axis), value)  191 us
    ppermute x7, waiting for transfers between devices, sent_to_each(): lax.ppermute(sent, axis, [(i, (i + step) % count) for i in range(count)])  149 us
    unnamed x25, local copies, waits for them, and re-layouts  39.1 us
    gather x1, local copies, waits for them, and re-layouts, body(): values = memory_values[offsets]  35.4 us
    gather x1, local copies, waits for them, and re-layouts, body(): memory_keys[offsets]  35.4 us
    dynamic_slice x24, local copies, waits for them, and re-layouts, body(): lax.map(score_source, (source_queries, picked_keys, local_rows, source_pe...  21.7 us
    dynamic_update_slice x7, local copies, waits for them, and re-layouts, sent_to_each(): out = lax.dynamic_update_slice_in_dim(out, other, source, axis=0)  21.7 us
    ppermute x7, starting transfers between devices, sent_to_each(): lax.ppermute(sent, axis, [(i, (i + step) % count) for i in range(count)])  18.5 us
  transfers between devices with their start and end apart: 11, of which 3 were waited for; matrix products, arithmetic and copies ran while one was open for 40% of the time, Pallas kernels for 0%

profile of v1, /device:TPU:0, one launch (start us, length us, event | category | flops | bytes accessed | tf_op | source)
XLA Modules:
  0.0 655.2 jit_solution(14052983296889186038)
XLA Ops:
  11.6 16.1 %scatter_custom_fusion = s32[8192]{0:T(1024)} fusion(s32[4096]{0:T(1024)S(1)} %bitcast.199, s32[4096]{0:T(1024)S(1)} %get-tuple-element.214, s32[]{:T(128)} %constant.215.clone.1), kind=kCustom, calls=%fused_computation.120 | custom fusion | bytes 32772 | tf_op jit(solution)/shard_map/scatter | solution.py:119
  27.7 7.3 %all-to-all-start = ((s32[8,1,1024]{2,1,0:T(1,128)}), s32[8,1,1024]{2,1,0:T(1,128)S(1)}, u32[]{:S(2)}, u32[]{:S(2)}) async-start(s32[8,1,1024]{2,1,0:T(1,128)} %bitcast.9), calls=%async_computation | async-start | bytes 65536 | tf_op jit(solution)/shard_map/all_to_all | solution.py:125
  41.9 35.4 %gather_fusion = bf16[8192,1024]{1,0:T(8,128)(2,1)} fusion(bf16[1024,1024]{1,0:T(8,128)(2,1)S(1)} %copy-done, s32[8192]{0:T(1024)S(1)} %broadcast_clamp_fusion), kind=kCustom, calls=%fused_computation | custom fusion | bytes 33587200 | tf_op jit(solution)/shard_map/gather | solution.py:132
  77.3 11.0 %dynamic-slice_bitcast_fusion.1 = (bf16[1,1,1024,1024]{3,2,0,1:T(8,128)(2,1)}, bf16[1,1,1024,1024]{3,2,0,1:T(8,128)(2,1)}, bf16[1,1,1024,1024]{3,2,0,1:T(8,128)(...) fusion(bf16[8,1024,1024]{2,1,0:T(8,128)(2,1)} %bitcast.176, ...), kind=kLoop, calls=%fused_computation.41 | loop fusion | bytes 29360156 | tf_op jit(solution)/shard_map/jit(dynamic_index_in_dim)/dynamic_slice | solution.py:26
  88.8 15.5 %scatter_custom_fusion.1 = s32[8192]{0:T(1024)S(1)} fusion(s32[4096]{0:T(1024)S(1)} %bitcast.200, s32[4096]{0:T(1024)S(1)} %add_select_fusion.2, s32[]{:T(128)} %constant.215.clone.1), kind=kCustom, calls=%fused_computation.118 | custom fusion | bytes 32772 | tf_op jit(solution)/shard_map/scatter | solution.py:123
  104.4 2.6 copy.65
  106.9 3.9 copy.67
  119.6 35.4 %gather_fusion.1 = bf16[8192,1024]{1,0:T(8,128)(2,1)} fusion(bf16[1024,1024]{1,0:T(8,128)(2,1)S(1)} %copy-done.2, s32[8192]{0:T(1024)S(1)} %broadcast_clamp_fusion), kind=kCustom, calls=%fused_computation.1 | custom fusion | bytes 33587200 | tf_op jit(solution)/shard_map/gather | solution.py:131
  155.0 15.6 %copy.87 = bf16[1024,8,8,128]{3,2,1,0:T(8,128)(2,1)} copy(bf16[1024,8,8,128]{3,1,2,0:T(8,128)(2,1)} %bitcast.180) | data formatting | bytes 33554432
  172.2 3.1 constant_dynamic-update-slice_fusion.6
  175.3 9.2 %collective-permute-start.6 = (bf16[1,1,1024,1024]{3,2,0,1:T(8,128)(2,1)}, bf16[1,1,1024,1024]{3,2,0,1:T(8,128)(2,1)}, u32[]{:S(2)}, u32[]{:S(2)}) collective-permute-start(bf16[1,1,1024,1024]{3,2,0,1:T(8,128)(2,1)} %get-tuple-element.207), channel_id=1, source_target_pairs={{0,28},{4,0},{8,4},{12,8},{16,12},{20,16},{24,20},{28,24},{1,29},{... | collective-permute-start | bytes 6291464 | tf_op jit(solution)/shard_map/ppermute | solution.py:27
  184.5 3.1 constant_dynamic-update-slice_fusion.5
  187.6 129.5 %collective-permute-done.2 = bf16[1,1,1024,1024]{3,2,0,1:T(8,128)(2,1)} collective-permute-done((bf16[1,1,1024,1024]{3,2,0,1:T(8,128)(2,1)}, bf16[1,1,1024,1024]{3,2,0,1:T(8,128)(2,1)}, u32[]{:S(2)}, u32[]{:S(2)}) %collective-permute-start.2) | collective-permute-done | bytes 2097184 | tf_op jit(solution)/shard_map/ppermute | solution.py:27
  317.1 3.1 constant_dynamic-update-slice_fusion.4
  320.2 19.8 %collective-permute-done.3 = bf16[1,1,1024,1024]{3,2,0,1:T(8,128)(2,1)} collective-permute-done((bf16[1,1,1024,1024]{3,2,0,1:T(8,128)(2,1)}, bf16[1,1,1024,1024]{3,2,0,1:T(8,128)(2,1)}, u32[]{:S(2)}, u32[]{:S(2)}) %collective-permute-start.3) | collective-permute-done | bytes 2097184 | tf_op jit(solution)/shard_map/ppermute | solution.py:27
  340.0 3.2 constant_dynamic-update-slice_fusion.3
  343.1 3.1 constant_dynamic-update-slice_fusion.2
  346.2 19.3 %while.35 = (s32[]{:T(128)}, f32[2,512,8]{1,2,0:T(8,128)S(1)}, f32[2,512,8]{1,2,0:T(8,128)S(1)}, bf16[2,512,1024]{2,1,0:T(8,128)(2,1)}, bf16[1024,8,128]{2,0,1:T(8,128)(2,1)}, /*index=5*/s32[]{:T(128)}) while((s32[]{:T(128)}, f32[2,512,8]{1,2,0:T(8,128)S(1)}, f32[2,512,8]{1,2,0:T(8,128)S(1)}, bf16[2,512,1024]{2,1,0:T(8,128)(2,1)}, ...), condition=%wide.region_8.9_spmd, body=%wide.region_5.8_spmd.sunk | while | flops 1094705152 | bytes 41009236 | solution.py:102
  348.1 4.2 bitcast_reduce_fusion.2
  352.3 3.5 fusion.82
  357.7 4.2 bitcast_reduce_fusion.2
  361.9 3.5 fusion.82
  365.5 160.1 %all_gather.13 = f32[8,1024,8]{1,2,0:T(8,128)S(1)} all-gather(f32[1,1024,8]{1,2,0:T(8,128)S(1)} %bitcast.196), channel_id=1, replica_groups=mesh['mem'=8,'pb'=4] {'mem'}, dimensions={0}, use_global_device_ids=true | all-gather | bytes 294912 | tf_op jit(solution)/shard_map/all_gather | solution.py:33
  525.6 30.7 %all_gather.14 = f32[8,1024,8]{1,2,0:T(8,128)S(1)} all-gather(f32[1,1024,8]{1,2,0:T(8,128)S(1)} %bitcast.197), channel_id=1, replica_groups=mesh['mem'=8,'pb'=4] {'mem'}, dimensions={0}, use_global_device_ids=true | all-gather | bytes 294912 | tf_op jit(solution)/shard_map/all_gather | solution.py:33
  556.4 3.5 copy.86
  560.3 43.2 %while.37 = (s32[]{:T(128)}, bf16[8,1024,8]{1,2,0:T(8,128)(2,1)}, s32[8,1024]{1,0:T(8,128)S(1)}, bf16[8,128,8,128]{3,2,1,0:T(8,128)(2,1)}, bf16[8,1024,8,128]{3,...) while((s32[]{:T(128)}, bf16[8,1024,8]{1,2,0:T(8,128)(2,1)}, ...), condition=%wide.region_14.15_spmd.clone, body=%wide.region_11.14_spmd.clone.sunk | while | flops 273818624 | bytes 7657577 | solution.py:146
  603.5 6.0 all-to-all-start.1
  609.5 3.1 constant_dynamic-update-slice_fusion.1
  612.5 3.1 constant_dynamic-update-slice_fusion
  615.6 15.6 %copy.85 = bf16[1024,8,8,128]{3,2,1,0:T(8,128)(2,1)} copy(bf16[1024,8,8,128]{3,1,2,0:T(8,128)(2,1)} %bitcast.178) | data formatting | bytes 33554432
  632.0 11.9 %fusion.33 = f32[128,8,128]{0,2,1:T(8,128)} fusion(pred[128,8192]{1,0:T(8,128)(4,1)S(1)} %iota_compare_fusion.1, bf16[8,8192]{1,0:T(8,128)(2,1)} %bitcast.193, bf16[8192,8,128]{2,1,0:T(8,128)(2,1)} %bitcast.184, f32[128,8]{0,1:T(8,128)S(1)} %convolution_add_fusion, f32[8]{0:T(128)S(1)} %copy-done.9), kind=kOutput, calls=%fused_computation.57 | convolution fusion | flops 2156134400 | bytes 18485280 | tf_op jit(solution)/shard_map/hqs,shd->qhd/dot_general | solution.py:156
  645.6 2.8 convolution_convert_fusion
  (166 shorter events, 72.2 us)
Async XLA Ops:
  6.5 35.3 %copy-start = (bf16[1024,1024]{1,0:T(8,128)(2,1)S(1)}, bf16[1024,1024]{1,0:T(8,128)(2,1)}, u32[]{:S(2)}) copy-start(bf16[1024,1024]{1,0:T(8,128)(2,1)} %param.18) | copy-start | bytes 6291460
  6.5 339.7 %all-gather.3.cloned.1.call-start = ((), (), s32[]{:S(2)}) async-start(), calls=%async_computation.2 | async-start | bytes 2359296 | tf_op jit(solution)/shard_map/all_gather | solution.py:72
  27.7 14.0 %all-to-all-start = ((s32[8,1,1024]{2,1,0:T(1,128)}), s32[8,1,1024]{2,1,0:T(1,128)S(1)}, u32[]{:S(2)}, u32[]{:S(2)}) async-start(s32[8,1,1024]{2,1,0:T(1,128)} %bitcast.9), calls=%async_computation | async-start | bytes 65536 | tf_op jit(solution)/shard_map/all_to_all | solution.py:125
  34.9 610.7 %all-gather.5.cloned.1.call-start = ((), (), s32[]{:S(2)}) async-start(), calls=%async_computation.3 | async-start | bytes 2621440 | tf_op jit(solution)/shard_map/all_gather | solution.py:171
  38.3 0.8 copy-start.3
  77.3 27.0 %copy-start.2 = (bf16[1024,1024]{1,0:T(8,128)(2,1)S(1)}, bf16[1024,1024]{1,0:T(8,128)(2,1)}, u32[]{:S(2)}) copy-start(bf16[1024,1024]{1,0:T(8,128)(2,1)} %param.17) | copy-start | bytes 6291460
  88.3 82.4 %collective-permute-start = (bf16[1,1,1024,1024]{3,2,0,1:T(8,128)(2,1)}, bf16[1,1,1024,1024]{3,2,0,1:T(8,128)(2,1)}, u32[]{:S(2)}, u32[]{:S(2)}) collective-permute-start(bf16[1,1,1024,1024]{3,2,0,1:T(8,128)(2,1)} %get-tuple-element.212), channel_id=1, source_target_pairs={{0,4},{4,8},{8,12},{12,16},{16,20},{20,24},{24,28},{28,0},{1,5},{5... | collective-permute-start | bytes 6291464 | tf_op jit(solution)/shard_map/ppermute | solution.py:27
  104.3 6.5 copy-start.4
  111.7 63.6 %collective-permute-start.1 = (bf16[1,1,1024,1024]{3,2,0,1:T(8,128)(2,1)}, bf16[1,1,1024,1024]{3,2,0,1:T(8,128)(2,1)}, u32[]{:S(2)}, u32[]{:S(2)}) collective-permute-start(bf16[1,1,1024,1024]{3,2,0,1:T(8,128)(2,1)} %get-tuple-element.211), channel_id=1, source_target_pairs={{0,8},{4,12},{8,16},{12,20},{16,24},{20,28},{24,0},{28,4},{1,9},{5... | collective-permute-start | bytes 6291464 | tf_op jit(solution)/shard_map/ppermute | solution.py:27
  112.9 204.2 %collective-permute-start.2 = (bf16[1,1,1024,1024]{3,2,0,1:T(8,128)(2,1)}, bf16[1,1,1024,1024]{3,2,0,1:T(8,128)(2,1)}, u32[]{:S(2)}, u32[]{:S(2)}) collective-permute-start(bf16[1,1,1024,1024]{3,2,0,1:T(8,128)(2,1)} %get-tuple-element.210), channel_id=1, source_target_pairs={{0,12},{4,16},{8,20},{12,24},{16,28},{20,0},{24,4},{28,8},{1,13},{... | collective-permute-start | bytes 6291464 | tf_op jit(solution)/shard_map/ppermute | solution.py:27
  115.3 224.7 %collective-permute-start.3 = (bf16[1,1,1024,1024]{3,2,0,1:T(8,128)(2,1)}, bf16[1,1,1024,1024]{3,2,0,1:T(8,128)(2,1)}, u32[]{:S(2)}, u32[]{:S(2)}) collective-permute-start(bf16[1,1,1024,1024]{3,2,0,1:T(8,128)(2,1)} %get-tuple-element.209), channel_id=1, source_target_pairs={{0,16},{4,20},{8,24},{12,28},{16,0},{20,4},{24,8},{28,12},{1,17},{... | collective-permute-start | bytes 6291464 | tf_op jit(solution)/shard_map/ppermute | solution.py:27
  116.9 226.3 %collective-permute-start.4 = (bf16[1,1,1024,1024]{3,2,0,1:T(8,128)(2,1)}, bf16[1,1,1024,1024]{3,2,0,1:T(8,128)(2,1)}, u32[]{:S(2)}, u32[]{:S(2)}) collective-permute-start(bf16[1,1,1024,1024]{3,2,0,1:T(8,128)(2,1)} %get-tuple-element.208), channel_id=1, source_target_pairs={{0,20},{4,24},{8,28},{12,0},{16,4},{20,8},{24,12},{28,16},{1,21},{... | collective-permute-start | bytes 6291464 | tf_op jit(solution)/shard_map/ppermute | solution.py:27
  170.7 438.7 %collective-permute-start.5 = (bf16[1,1,1024,1024]{3,2,0,1:T(8,128)(2,1)}, bf16[1,1,1024,1024]{3,2,0,1:T(8,128)(2,1)}, u32[]{:S(2)}, u32[]{:S(2)}) collective-permute-start(bf16[1,1,1024,1024]{3,2,0,1:T(8,128)(2,1)} %get-tuple-element.213), channel_id=1, source_target_pairs={{0,24},{4,28},{8,0},{12,4},{16,8},{20,12},{24,16},{28,20},{1,25},{... | collective-permute-start | bytes 6291464 | tf_op jit(solution)/shard_map/ppermute | solution.py:27
  175.3 437.2 %collective-permute-start.6 = (bf16[1,1,1024,1024]{3,2,0,1:T(8,128)(2,1)}, bf16[1,1,1024,1024]{3,2,0,1:T(8,128)(2,1)}, u32[]{:S(2)}, u32[]{:S(2)}) collective-permute-start(bf16[1,1,1024,1024]{3,2,0,1:T(8,128)(2,1)} %get-tuple-element.207), channel_id=1, source_target_pairs={{0,28},{4,0},{8,4},{12,8},{16,12},{20,16},{24,20},{28,24},{1,29},{... | collective-permute-start | bytes 6291464 | tf_op jit(solution)/shard_map/ppermute | solution.py:27
  603.5 27.8 %all-to-all-start.1 = ((bf16[8,1024,8]{1,2,0:T(8,128)(2,1)}), bf16[8,1024,8]{1,2,0:T(8,128)(2,1)S(1)}, u32[]{:S(2)}, u32[]{:S(2)}) async-start(bf16[8,1024,8]{1,2,0:T(8,128)(2,1)} %get-tuple-element.101), calls=%async_computation.1 | async-start | bytes 262144 | tf_op jit(solution)/shard_map/all_to_all | solution.py:150
  615.6 16.4 %copy-start.9 = (f32[8]{0:T(128)S(1)}, f32[8]{0:T(128)}, u32[]{:S(2)}) copy-start(f32[8]{0:T(128)} %get-tuple-element.202) | copy-start | bytes 100
  631.2 0.7 copy-start.6
  632.0 11.9 %copy-start.5 = (bf16[128,1024]{0,1:T(8,128)(2,1)S(1)}, bf16[128,1024]{0,1:T(8,128)(2,1)}, u32[]{:S(2)}) copy-start(bf16[128,1024]{0,1:T(8,128)(2,1)} %copy.77) | copy-start | bytes 786436
  632.0 11.9 %copy-start.7 = (f32[8,128]{1,0:T(8,128)S(1)}, f32[8,128]{1,0:T(8,128)}, u32[]{:S(2)}) copy-start(f32[8,128]{1,0:T(8,128)} %fusion.64) | copy-start | bytes 12292
  632.0 11.9 %copy-start.8 = (f32[8]{0:T(128)S(1)}, f32[8]{0:T(128)}, u32[]{:S(2)}) copy-start(f32[8]{0:T(128)} %get-tuple-element.201) | copy-start | bytes 100
  632.0 16.4 %copy-start.1 = (bf16[1024,1024]{1,0:T(8,128)(2,1)S(1)}, bf16[1024,1024]{1,0:T(8,128)(2,1)}, u32[]{:S(2)}) copy-start(bf16[1024,1024]{1,0:T(8,128)(2,1)} %param.18) | copy-start | bytes 6291460
Sparse Core Ops, SparseCore 0:
  9.5 51.9 all-gather.2
  63.1 21.0 all-gather.4
